TPU v7x, 128 devices: a whole 4x4x4 slice. The times are simulated.
128 devices in a mesh: rows: 64 (over z, x, y), sub: 2 (over core).
Axes of the slice: x: 4, y: 4, z: 4, core: 2. Of those that a mesh axis runs over, the one named last changes fastest.
Arguments:
- points: bfloat16 [49152, 128], P('rows'), may hold values from -5 to 5, as said below
- old_factor: float32 [49152, 512], P('rows', 'sub'), may hold values from -0.039774756 to 0.039774756
- targets: float32 [49152], P('rows'), may hold values from -6 to 6
- pivots: int32 [512], replicated, may hold values from 0 to 49151, as said below
Outputs:
- new_factor: float32 [49152, 512], P('rows', 'sub')
- solution: float32 [49152], P('rows')
- residual: float32 [49152], P('rows')
- preconditioned: float32 [49152], P('rows')
Inputs may be any that keep to these rules, and one draw needn't show every extreme that they name: `points`: cluster centres plus small per-point offsets. `pivots`: 512 distinct point indices.
All inputs are finite; a program needn't handle non-finite values.
Results may differ from a plain program's by a relative error of at most 0.0018.
Values may be sent and summed in bfloat16 or wider, within the bound.
No kernel may reach another device: no remote copies, remote signals or barrier semaphores. Data moves between devices by JAX's collectives and lax.ppermute only.
A program may use at most 128 MiB of HBM per device.

v0:
```python
import jax
import jax.numpy as jnp
from jax import lax
from jax.sharding import PartitionSpec as P

ridge_shift = 0.5
precise = lax.Precision.HIGHEST


def kernel_values(left, left_norms, right, right_norms):
    inner = lax.dot_general(
        left, right, (((1,), (1,)), ((), ())), preferred_element_type=jnp.float32
    )
    dist = jnp.maximum(left_norms[:, None] + right_norms[None, :] - 2.0 * inner, 0.0)
    return jnp.exp(-(2.0 / left.shape[1]) * dist)


def point_norms(rows):
    wide = rows.astype(jnp.float32)
    return jnp.sum(wide * wide, axis=1)


def precondition(vector, factor, core_lower, projection):
    coef = jax.scipy.linalg.cho_solve((core_lower, True), projection)
    return (vector - jnp.dot(factor, coef, precision=precise)) / ridge_shift


def local(points, old_factor, targets, pivots):
    count = points.shape[0]
    parts = lax.axis_size("sub")
    part = lax.axis_index("sub")
    half = count // parts
    first = lax.axis_index("rows") * count
    old_full = lax.all_gather(old_factor, "sub", axis=1, tiled=True)
    row_ids = first + lax.iota(jnp.int32, count)
    picks = row_ids[:, None] == pivots[None, :]
    pick_points = lax.dot_general(
        picks.astype(jnp.bfloat16),
        points,
        (((0,), (0,)), ((), ())),
        preferred_element_type=jnp.float32,
    )
    pick_old = lax.dot_general(
        picks.astype(jnp.float32), old_full, (((0,), (0,)), ((), ())), precision=precise
    )
    pivot_points, pivot_old = lax.psum((pick_points, pick_old), "rows")
    pivot_narrow = pivot_points.astype(jnp.bfloat16)
    norms = point_norms(points)
    pivot_norms = jnp.sum(pivot_points * pivot_points, axis=1)
    columns = kernel_values(points, norms, pivot_narrow, pivot_norms) - jnp.dot(
        old_full, pivot_old.T, precision=precise
    )
    pivot_count = pivot_points.shape[0]
    block = kernel_values(pivot_narrow, pivot_norms, pivot_narrow, pivot_norms) - jnp.dot(
        pivot_old, pivot_old.T, precision=precise
    )
    block = block + ridge_shift * jnp.eye(pivot_count, dtype=jnp.float32)
    lower = jnp.linalg.cholesky(block)
    inverse = jax.scipy.linalg.solve_triangular(
        lower, jnp.eye(pivot_count, dtype=jnp.float32), lower=True
    )
    new_full = jnp.dot(columns, inverse.T, precision=precise)
    factor = jnp.concatenate([old_full, new_full], axis=1)
    width = factor.shape[1]
    owned = lax.dynamic_slice_in_dim(factor, part * (width // parts), width // parts, 1)
    gram_part = jnp.dot(factor.T, owned, precision=precise)
    proj_part = jnp.dot(targets, owned, precision=precise)
    gram_part, proj_part = lax.psum((gram_part, proj_part), "rows")
    gram, projection = (
        lax.all_gather(gram_part, "sub", axis=1, tiled=True),
        lax.all_gather(proj_part, "sub", axis=0, tiled=True),
    )
    core = gram + ridge_shift * jnp.eye(width, dtype=jnp.float32)
    core_lower = jnp.linalg.cholesky(core)
    direction = precondition(targets, factor, core_lower, projection)
    direction_full = lax.all_gather(direction, "rows", axis=0, tiled=True)
    weight_grid = direction_full.reshape(-1, count)
    empty = jnp.zeros((count,), jnp.float32)
    rows_block = lax.all_gather(points, "rows", axis=0, tiled=True)
    shards = rows_block.shape[0] // count
    blocks = lax.dynamic_slice_in_dim(
        rows_block.reshape(shards, count, rows_block.shape[1]), part * half, half, 1
    )
    weights = weight_grid
    weights = lax.dynamic_slice_in_dim(weights, part * half, half, 1)
    total = empty

    def one_block(acc, item):
        tile = kernel_values(points, norms, item[0], point_norms(item[0]))
        return (acc + jnp.dot(tile, item[1], precision=precise), None)

    total, unused = lax.scan(one_block, total, (blocks, weights))
    image = lax.psum(total, "sub") + ridge_shift * direction
    along_targets = lax.psum(jnp.sum(direction * targets), "rows")
    along_image = lax.psum(jnp.sum(direction * image), "rows")
    alpha = along_targets / along_image
    solution = alpha * direction
    residual = targets - alpha * image
    proj_residual = lax.psum(jnp.dot(residual, factor, precision=precise), "rows")
    preconditioned = precondition(residual, factor, core_lower, proj_residual)
    new_part = lax.dynamic_slice_in_dim(
        new_full, part * (pivot_count // parts), pivot_count // parts, 1
    )
    return (new_part, solution, residual, preconditioned)


def solution(mesh):
    in_specs = (P("rows", None), P("rows", "sub"), P("rows"), P())
    out_specs = (P("rows", "sub"), P("rows"), P("rows"), P("rows"))
    return jax.shard_map(local, mesh=mesh, in_specs=in_specs, out_specs=out_specs, check_vma=False)
```

profile of v0, /device:TPU:8, one launch (start us, length us, event | category | flops | bytes accessed | tf_op | source)
XLA Modules:
  0.0 1837.9 jit_solution(9491646269393277952)
XLA Ops:
  9.6 2.4 fusion.12
  12.0 13.1 all-gather.6.cloned.1.call-done
  25.1 4.2 fusion.104
  31.7 129.3 %all-reduce.9.cloned.1.call-done = (f32[512,512]{1,0:T(8,128)}, f32[512,128]{1,0:T(8,128)}) async-done(((f32[512,512]{1,0:T(8,128)}, f32[512,128]{1,0:T(8,128)}), (f32[512,512]{1,0:T(8,128)}, f32[512,128]{1,0:T(8,128)})) %all-reduce.9.cloned.1.call-update) | async-done | bytes 1310736 | tf_op jit(solution)/shard_map/psum | solution.py:46
  162.2 2.5 fusion.201
  164.7 3.4 fusion.315
  171.9 2.5 copy.22
  177.7 11.7 cholesky.278
  189.4 9.8 custom-call.84
  201.9 12.1 cholesky.292
  214.0 9.8 custom-call.85
  225.4 11.7 cholesky.313
  237.9 9.8 custom-call.86
  249.3 11.7 cholesky.328
  265.0 2.5 select_select_fusion.1
  267.6 14.0 while.16
  268.2 2.9 bitcast_dynamic-update-slice_fusion.4
  271.7 2.9 bitcast_dynamic-update-slice_fusion.4
  275.2 2.9 bitcast_dynamic-update-slice_fusion.4
  278.7 2.8 bitcast_dynamic-update-slice_fusion.4
  281.6 40.1 %custom-call.74 = f32[4,128,128]{1,2,0:T(8,128)S(1)} custom-call(f32[4,128,128]{2,1,0:T(8,128)} %get-tuple-element.56), custom_call_target="InvertDiagBlocksLowerTriangular" | custom-call | tf_op jit(solution)/shard_map/jit(_solve_triangular)/triangular_solve | solution.py:59
  328.6 2.7 fusion.314
  331.3 3.2 fusion.15
  334.5 7.0 fusion.24
  341.6 130.0 %all-reduce.7.cloned.1.call-done = f32[1024,512]{1,0:T(8,128)} async-done(((f32[1024,512]{1,0:T(8,128)}), f32[1024,512]{1,0:T(8,128)}) %all-reduce.7.cloned.1.call-update) | async-done | bytes 2097168 | tf_op jit(solution)/shard_map/psum | solution.py:68
  477.6 174.7 %psum.59 = f32[512]{0:T(512)S(1)} all-reduce(f32[512]{0:T(512)S(1)} %bitcast.746), channel_id=1, replica_groups=mesh['rows'=64,'sub'=2] {'rows'}, use_global_device_ids=true, to_apply=%region_29.33 | all-reduce | flops 512 | bytes 4096 | tf_op jit(solution)/shard_map/psum | solution.py:68
  654.1 4.8 select_add_fusion.1
  659.0 5.4 copy.27
  664.3 4.4 fusion.11
  670.7 11.7 cholesky.585
  682.4 2.6 cholesky.610
  685.6 9.8 custom-call.75
  695.4 2.4 constant_dynamic-update-slice_fusion.86
  700.1 11.9 cholesky.603
  713.1 9.8 custom-call.76
  727.8 13.2 cholesky.624
  743.1 11.3 custom-call.77
  759.4 12.7 cholesky.643
  773.4 10.6 custom-call.78
  787.5 11.7 cholesky.662
  800.4 10.2 custom-call.87
  813.9 11.7 cholesky.678
  826.3 9.8 custom-call.88
  839.1 11.9 cholesky.694
  851.6 9.8 custom-call.89
  864.1 11.7 cholesky.708
  886.8 4.9 select_select_fusion
  891.7 28.0 %while.18 = (s32[]{:T(128)}, f32[1024,1024]{1,0:T(8,128)}, s32[8,2]{0,1:T(2,128)S(1)}, f32[8,128,128]{2,1,0:T(8,128)}, s32[]{:T(128)}) while((s32[]{:T(128)}, f32[1024,1024]{1,0:T(8,128)}, s32[8,2]{0,1:T(2,128)S(1)}, f32[8,128,128]{2,1,0:T(8,128)}, s32[]{:T(128)}) %tuple.137), condition=%wide.while_cond, body=%wide.while_body.sunk | while | flops 2 | bytes 132205 | solution.py:24
  892.3 2.9 bitcast_dynamic-update-slice_fusion.5
  895.8 2.9 bitcast_dynamic-update-slice_fusion.5
  899.3 2.9 bitcast_dynamic-update-slice_fusion.5
  902.8 2.9 bitcast_dynamic-update-slice_fusion.5
  906.3 2.9 bitcast_dynamic-update-slice_fusion.5
  909.8 2.9 bitcast_dynamic-update-slice_fusion.5
  913.4 2.9 bitcast_dynamic-update-slice_fusion.5
  916.9 2.8 bitcast_dynamic-update-slice_fusion.5
  919.7 80.2 %custom-call.90 = f32[8,128,128]{1,2,0:T(8,128)} custom-call(f32[8,128,128]{2,1,0:T(8,128)} %get-tuple-element.84), custom_call_target="InvertDiagBlocksLowerTriangular" | custom-call | tf_op jit(solution)/shard_map/jit(_cho_solve)/triangular_solve | solution.py:24
  1036.1 173.3 %all-gather.1 = f32[64,1,768]{2,1,0:T(1,128)S(1)} all-gather(f32[1,1,768]{2,1,0:T(1,128)S(1)} %reshape.324), channel_id=1, replica_groups=mesh['rows'=64,'sub'=2] {'rows'}, dimensions={0}, use_global_device_ids=true | all-gather | bytes 199680 | tf_op jit(solution)/shard_map/all_gather | solution.py:76
  1209.5 6.2 constant_dynamic-slice_fusion.3
  1215.7 224.6 %while.17 = (s32[]{:T(128)}, f32[768]{0:T(1024)S(1)}, f32[768]{0:T(1024)S(1)}, bf16[64,384,128]{2,1,0:T(8,128)(2,1)}, bf16[768,128]{1,0:T(8,128)(2,1)S(1)}, /*index=5*/f32[64,384]{1,0:T(8,128)S(1)}, s32[]{:T(128)}, s32[]{:T(128)}) while((s32[]{:T(128)}, f32[768]{0:T(1024)S(1)}, f32[768]{0:T(1024)S(1)}, ...), condition=%wide.region_34.39_spmd.clone, body=%wide.region_32.38_spmd.clone.sunk | while | flops 80659584 | bytes 2772595 | solution.py:92
  1440.4 2.5 psum.61
  1443.4 172.3 %all-reduce.2 = (f32[]{:T(128)}, f32[]{:T(128)}) all-reduce(f32[]{:T(128)} %get-tuple-element.95, f32[]{:T(128)} %get-tuple-element.94), channel_id=1, replica_groups=mesh['rows'=64,'sub'=2] {'rows'}, use_global_device_ids=true, to_apply=%region_31.36 | all-reduce | flops 2 | bytes 16 | tf_op jit(solution)/shard_map/psum | solution.py:94
  1617.7 2.7 fusion.22
  1620.4 174.0 %psum.63 = f32[1024]{0:T(1024)S(1)} all-reduce(f32[1024]{0:T(1024)S(1)} %bitcast.739), channel_id=1, replica_groups=mesh['rows'=64,'sub'=2] {'rows'}, use_global_device_ids=true, to_apply=%region_38.43 | all-reduce | flops 1024 | bytes 8192 | tf_op jit(solution)/shard_map/psum | solution.py:99
  (525 shorter events, 378.7 us)
Async XLA Ops:
  7.2 23.2 %copy-start.8 = (bf16[768,128]{1,0:T(8,128)(2,1)S(1)}, bf16[768,128]{1,0:T(8,128)(2,1)}, u32[]{:S(2)}) copy-start(bf16[768,128]{1,0:T(8,128)(2,1)} %param.14) | copy-start | bytes 589828
  7.2 18.0 all-gather.6.cloned.1.call-start
  9.6 151.5 %all-reduce.9.cloned.1.call-start = ((), (), s32[]{:S(2)}) async-start(), calls=%async_computation.4 | async-start | bytes 2621440 | tf_op jit(solution)/shard_map/psum | solution.py:46
  29.4 442.2 %all-reduce.7.cloned.1.call-start = ((), (), s32[]{:S(2)}) async-start(), calls=%async_computation.1 | async-start | bytes 4194304 | tf_op jit(solution)/shard_map/psum | solution.py:68
  161.0 7.4 copy-start.6
  176.6 1.0 copy-start.5
  261.1 3.9 copy-start.3
  265.0 63.6 %copy-start = (f32[768,512]{0,1:T(8,128)S(1)}, f32[768,512]{0,1:T(8,128)}, u32[]{:S(2)}) copy-start(f32[768,512]{0,1:T(8,128)} %all-gather.6.cloned.1.call-done) | copy-start | bytes 4718596
  265.0 63.6 %copy-start.2 = (f32[512,512]{1,0:T(8,128)S(1)}, f32[512,512]{1,0:T(8,128)}, u32[]{:S(2)}) copy-start(f32[512,512]{1,0:T(8,128)} %get-tuple-element.126) | copy-start | bytes 3145732
  324.1 7.2 copy-start.4
  341.5 130.7 %copy-start.10 = (f32[768]{0:T(1024)S(1)}, f32[768]{0:T(1024)}, u32[]{:S(2)}) copy-start(f32[768]{0:T(1024)} %param.16) | copy-start | bytes 9220
  341.6 312.5 %all-gather.8.cloned.1.call-start = ((), (), s32[]{:S(2)}) async-start(), calls=%async_computation.2 | async-start | bytes 6291456 | tf_op jit(solution)/shard_map/all_gather | solution.py:70
  471.6 737.9 %all-gather.10.cloned.1.call-start = ((), (), s32[]{:S(2)}) async-start(), calls=%async_computation.3 | async-start | bytes 12779520 | tf_op jit(solution)/shard_map/all_gather | solution.py:79
  668.8 2.0 copy-start.1
  699.3 0.8 copy-start.7
  810.6 65.3 %copy-start.12 = (f32[128]{0:T(128)S(1)}, f32[128]{0:T(128)}, u32[]{:S(2)}) copy-start(f32[128]{0:T(128)} %get-tuple-element.155) | copy-start | bytes 1540
  810.6 65.9 %copy-start.13 = (f32[128]{0:T(128)S(1)}, f32[128]{0:T(128)}, u32[]{:S(2)}) copy-start(f32[128]{0:T(128)} %get-tuple-element.152) | copy-start | bytes 1540
  810.6 67.8 %copy-start.14 = (f32[128]{0:T(128)S(1)}, f32[128]{0:T(128)}, u32[]{:S(2)}) copy-start(f32[128]{0:T(128)} %get-tuple-element.149) | copy-start | bytes 1540
  810.6 69.1 %copy-start.15 = (f32[128]{0:T(128)S(1)}, f32[128]{0:T(128)}, u32[]{:S(2)}) copy-start(f32[128]{0:T(128)} %get-tuple-element.146) | copy-start | bytes 1540
  810.6 70.4 %copy-start.16 = (f32[128]{0:T(128)S(1)}, f32[128]{0:T(128)}, u32[]{:S(2)}) copy-start(f32[128]{0:T(128)} %get-tuple-element.143) | copy-start | bytes 1540
  886.8 4.9 copy-start.17
  1209.5 6.2 copy-start.9
  1617.1 213.4 %copy-start.11 = (f32[768]{0:T(1024)}, f32[768]{0:T(1024)S(1)}, u32[]{:S(2)}) copy-start(f32[768]{0:T(1024)S(1)} %multiply_subtract_fusion) | copy-start | bytes 9220
Sparse Core Ops, SparseCore 0:
  10.2 14.8 all-gather.5
  30.1 130.8 all-reduce.8
  341.7 129.8 all-reduce.6
  473.2 15.3 all-gather.7
  491.6 92.5 all-gather.9
where the time goes:
time: 1850 us; the launch traced here: 1840 us
  blocking collectives  699 us (38%)
  other arithmetic  472 us (26%)
  matrix products  296 us (16%)
  waiting for transfers between devices  273 us (15%)
  local copies, waits for them, and re-layouts  72 us (4%)
  between operations  24.1 us (1%)
    another operation x31, other arithmetic, local(): core_lower = jnp.linalg.cholesky(core)  181 us
    psum x1, blocking collectives, local(): gram_part, proj_part = lax.psum((gram_part, proj_part), 'rows')  175 us
    psum x1, blocking collectives, local(): lax.psum(jnp.dot(residual, factor, precision=precise), 'rows')  174 us
    all_gather x1, blocking collectives, local(): direction_full = lax.all_gather(direction, 'rows', axis=0, tiled=True)  173 us
    psum x1, blocking collectives, local(): along_targets = lax.psum(jnp.sum(direction * targets), 'rows')  172 us
    psum x1, waiting for transfers between devices, local(): gram_part, proj_part = lax.psum((gram_part, proj_part), 'rows')  130 us
    psum x1, waiting for transfers between devices, local(): pivot_points, pivot_old = lax.psum((pick_points, pick_old), 'rows')  129 us
    dot_general x66, matrix products, kernel_values(): lax.dot_general(left, right, (((1,), (1,)), ((), ())), preferred_element_...  89.7 us
  transfers between devices with their start and end apart: 5, of which 3 were waited for; matrix products, arithmetic and copies ran while one was open for 21% of the time, Pallas kernels for 0%

commit v1 on v0

v1 whole, which is shorter than its diff:
```python
import math

import jax
import jax.numpy as jnp
from jax import lax
from jax.experimental import pallas as pl
from jax.experimental.pallas import tpu as pltpu
from jax.sharding import PartitionSpec as P

ridge_shift = 0.5
precise = lax.Precision.HIGHEST
everyone = ("rows", "sub")
f32, bf16 = jnp.float32, jnp.bfloat16


def factor_blocks(mats):
    lane = lax.broadcasted_iota(jnp.int32, (8, 128), 1)
    sub = lax.broadcasted_iota(jnp.int32, (8, 128), 0)
    outs = [[] for _ in mats]
    state = list(mats)
    for panel in range(16):
        lo = 8 * panel
        inside = (lane >= lo) & (lane < lo + 8)
        unit = (lane == lo + sub).astype(jnp.float32)
        cols = [[jnp.broadcast_to(a[:, lo + j:lo + j + 1], a.shape) for j in range(8)] for a in state]
        heads = [jnp.where(inside, unit, a[:8]) for a in state]
        scales = [jnp.zeros((8, 128), jnp.float32) for a in state]
        tails = [[] for _ in state]
        for j in range(8):
            for m in range(len(state)):
                col = cols[m][j]
                pivot = jnp.broadcast_to(col[j:j + 1], (8, 128))
                recip = 1.0 / pivot
                scales[m] = jnp.where(sub == j, lax.rsqrt(pivot), scales[m])
                top = jnp.where(sub > j, col[:8] * recip, 0.0)
                rest = col[8:] * recip[:1] if col.shape[0] > 8 else None
                for later in range(j + 1, 8):
                    row = cols[m][later][j:j + 1]
                    new = cols[m][later][:8] - top * row
                    if rest is not None:
                        new = jnp.concatenate([new, cols[m][later][8:] - rest * row], 0)
                    cols[m][later] = new
                heads[m] = heads[m] - top * heads[m][j:j + 1]
                tails[m].append(rest)
        for m in range(len(state)):
            outs[m].append(heads[m] * scales[m])
            if panel < 15:
                a = state[m][8:]
                inside_all = jnp.broadcast_to(inside[:1], a.shape)
                a = jnp.where(inside_all, 0.0, a)
                for j in range(8):
                    a = a - tails[m][j] * heads[m][j:j + 1]
                state[m] = a
    low = lax.broadcasted_iota(jnp.int32, (128, 128), 0) >= lax.broadcasted_iota(jnp.int32, (128, 128), 1)
    return [jnp.where(low, jnp.concatenate(o, 0), 0.0) for o in outs]

def chol_inverse(refs, size):
    rows = lax.broadcasted_iota(jnp.int32, (size, size), 0)
    colid = lax.broadcasted_iota(jnp.int32, (size, size), 1)
    crow = lax.broadcasted_iota(jnp.int32, (128, size), 1)
    def step(k, carry):
        off = pl.multiple_of(k * 128, 128)
        here = pl.ds(off, 128)
        invs = factor_blocks([r[here, here] for r in refs])
        inside = (crow >= off) & (crow < off + 128)
        inside_all = (colid >= off) & (colid < off + 128)
        for r, inv in zip(refs, invs):
            left = lax.dot_general(r[:, here], inv, (((1,), (1,)), ((), ())), precision=precise, preferred_element_type=jnp.float32)
            r[here, here] = inv
            head = jnp.dot(inv, jnp.where(inside, 0.0, r[here, :]), precision=precise, preferred_element_type=jnp.float32)
            r[here, :] = head
            r[here, here] = inv
            upd = jnp.dot(left, r[here, :], precision=precise, preferred_element_type=jnp.float32)
            old = r[...]
            r[...] = jnp.where(rows >= off + 128, jnp.where(inside_all, 0.0, old) - upd, old)
        return carry
    lax.fori_loop(0, size // 128, step, 0)
    for r in refs:
        r[...] = jnp.where(rows >= colid, r[...], 0.0)


def pair_kernel(first_in, second_in, first_out, second_out):
    first_out[...] = first_in[...]
    second_out[...] = second_in[...]
    chol_inverse([first_out, second_out], first_in.shape[0])


def single_kernel(matrix, out):
    out[...] = matrix[...]
    chol_inverse([out], matrix.shape[0])


def factor_pair(first, second):
    shape = jax.ShapeDtypeStruct(first.shape, f32)
    return pl.pallas_call(
        pair_kernel,
        out_shape=(shape, shape),
        compiler_params=pltpu.CompilerParams(vmem_limit_bytes=40 << 20),
        name="factor_pair",
    )(first, second)


def factor_single(matrix):
    return pl.pallas_call(
        single_kernel,
        out_shape=jax.ShapeDtypeStruct(matrix.shape, f32),
        compiler_params=pltpu.CompilerParams(vmem_limit_bytes=40 << 20),
        name="factor_single",
    )(matrix)


def rows_kernel(scale, left, points, shifts, weights, out, acc):
    @pl.when(pl.program_id(0) == 0)
    def _():
        acc[...] = jnp.zeros_like(acc)

    lane = lax.broadcasted_iota(jnp.int32, (256, 128), 1)
    ones = jnp.where(lane < 3, 1.0, 0.0).astype(bf16)
    total = acc[...]
    for tile in range(points.shape[0] // 256):
        here = slice(256 * tile, 256 * tile + 256)
        right = jnp.concatenate([points[here], ones], axis=1)
        inner = lax.dot_general(left[...], right, (((1,), (1,)), ((), ())), preferred_element_type=f32)
        value = jnp.exp2(jnp.minimum(inner * scale + shifts[:, here], 0.0)) * weights[:, here]
        total = total + (value[:, :128] + value[:, 128:])
    acc[...] = total

    @pl.when(pl.program_id(0) == pl.num_programs(0) - 1)
    def _():
        ones_row = jnp.ones((8, 128), f32)
        out[...] = lax.dot_general(
            ones_row, acc[...], (((1,), (1,)), ((), ())), precision=precise, preferred_element_type=f32
        )


def kernel_rows(points, norms, others, other_norms, weights):
    count, dim = points.shape
    scale = 2.0 * (2.0 / dim) * math.log2(math.e)
    half_norms = -0.5 * norms
    pieces = []
    for _ in range(3):
        piece = lax.reduce_precision(half_norms, 8, 7)
        pieces.append(piece.astype(bf16))
        half_norms = half_norms - piece
    extra = jnp.pad(jnp.stack(pieces, axis=1), ((0, 0), (0, dim - 3)))
    left = jnp.concatenate([points, extra], axis=1)
    shifts = (-0.5 * scale) * other_norms
    total = others.shape[0]
    steps = 8
    size = total // steps
    out = pl.pallas_call(
        lambda *refs: rows_kernel(scale, *refs),
        grid=(steps,),
        in_specs=[
            pl.BlockSpec((count, 2 * dim), lambda i: (0, 0)),
            pl.BlockSpec((size, dim), lambda i: (i, 0)),
            pl.BlockSpec((1, size), lambda i: (0, i)),
            pl.BlockSpec((1, size), lambda i: (0, i)),
        ],
        out_specs=pl.BlockSpec((8, count), lambda i: (0, 0)),
        out_shape=jax.ShapeDtypeStruct((8, count), f32),
        scratch_shapes=[pltpu.VMEM((count, 128), f32)],
        compiler_params=pltpu.CompilerParams(vmem_limit_bytes=40 << 20),
        name="kernel_rows",
    )(left, others, shifts[None], weights[None])
    return out[0]


def kernel_values(left, left_norms, right, right_norms):
    inner = lax.dot_general(left, right, (((1,), (1,)), ((), ())), preferred_element_type=f32)
    dist = jnp.maximum(left_norms[:, None] + right_norms[None, :] - 2.0 * inner, 0.0)
    return jnp.exp(-(2.0 / left.shape[1]) * dist)


def point_norms(rows):
    wide = rows.astype(f32)
    return jnp.sum(wide * wide, axis=1)


def dot(left, right, contract):
    return lax.dot_general(left, right, (contract, ((), ())), precision=precise, preferred_element_type=f32)


def exchange(pieces):
    return lax.all_to_all(pieces, everyone, 0, 0, tiled=True)


def spread(piece, parts):
    return exchange(jnp.broadcast_to(piece.reshape(1, -1), (parts, piece.size)))


def swap(value):
    return lax.ppermute(value, "sub", [(0, 1), (1, 0)])


def both(mine, part, axis):
    other = swap(mine)
    first = jnp.where(part == 0, mine, other)
    second = jnp.where(part == 0, other, mine)
    return jnp.concatenate([first, second], axis=axis)


def split(value):
    high = lax.reduce_precision(value, 8, 7)
    return high.astype(bf16), (value - high).astype(bf16)


def local(points, old_factor, targets, pivots):
    count, dim = points.shape
    pivot_count = pivots.shape[0]
    prev = 2 * old_factor.shape[1]
    part = lax.axis_index("sub")
    chips = lax.axis_size("rows")
    parts = 2 * chips
    half = count // 2
    each = pivot_count // parts
    first = lax.axis_index("rows") * count
    norms = point_norms(points)
    others = lax.all_gather(
        lax.dynamic_slice_in_dim(points, part * half, half, 0), "rows", axis=0, tiled=True
    )

    picks = (pivots[:, None] == (first + lax.iota(jnp.int32, count))[None, :]).astype(bf16)
    high, low = split(old_factor)
    my_points = lax.dynamic_slice_in_dim(points, part * (dim // 2), dim // 2, 1)
    wanted = jnp.concatenate([my_points, high, low], axis=1)
    picked = lax.dot_general(picks, wanted, (((1,), (0,)), ((), ())), preferred_element_type=f32)
    width = wanted.shape[1]
    came = exchange(picked.astype(bf16).reshape(parts, each * width))
    came = jnp.sum(came.reshape(chips, 2, each, width).astype(f32), axis=0).astype(bf16)
    kept = jnp.concatenate([came[0], came[1]], axis=1)
    pivot_rows = spread(kept, parts).reshape(pivot_count, 2 * width)
    cols = old_factor.shape[1]
    pivot_points = jnp.concatenate(
        [pivot_rows[:, : dim // 2], pivot_rows[:, width : width + dim // 2]], axis=1
    )

    def pivot_half(start):
        start = start + dim // 2
        return pivot_rows[:, start : start + cols].astype(f32) + pivot_rows[
            :, start + cols : start + 2 * cols
        ].astype(f32)

    pivot_old = jnp.concatenate([pivot_half(0), pivot_half(width)], axis=1)
    pivot_norms = point_norms(pivot_points)

    old_full = both(old_factor, part, 1)
    old_gram = dot(old_full, old_factor, ((0,), (0,)))
    old_gram = exchange(old_gram.reshape(parts, -1))
    old_gram = jnp.sum(old_gram.reshape(chips, 2, -1), axis=0)
    old_gram = spread(old_gram, parts).reshape(parts, 2, prev // parts, cols)
    old_gram = jnp.concatenate(
        [old_gram[:, 0].reshape(prev, cols), old_gram[:, 1].reshape(prev, cols)], axis=1
    )
    old_core = old_gram + ridge_shift * jnp.eye(prev, dtype=f32)

    columns = kernel_values(points, norms, pivot_points, pivot_norms) - dot(
        old_full, pivot_old, ((1,), (1,))
    )
    block = kernel_values(pivot_points, pivot_norms, pivot_points, pivot_norms) - dot(
        pivot_old, pivot_old, ((1,), (1,))
    )
    block = block + ridge_shift * jnp.eye(pivot_count, dtype=f32)

    side = jnp.where(part == 0, old_full, columns)
    gram = dot(side, columns, ((0,), (0,)))
    proj = jnp.sum(side * targets[:, None], axis=0)
    pad = 128 - prev // parts
    sent = jnp.concatenate(
        [gram.reshape(parts, -1), jnp.pad(proj.reshape(parts, -1), ((0, 0), (0, pad)))], axis=1
    )
    size = sent.shape[1]
    came = jnp.sum(exchange(sent).reshape(chips, 2, size), axis=0)
    came = exchange(jnp.broadcast_to(came[None], (chips, 2, size)).reshape(parts, size))
    came = both(came[None], part, 0)
    grams = came[:, :, : size - 128].reshape(2, prev, pivot_count)
    projs = came[:, :, size - 128 : size - pad].reshape(2, prev)
    cross, square = grams[0], grams[1]
    old_proj, new_proj = projs[0], projs[1]

    old_inverse, block_inverse = factor_pair(old_core, block)
    cross_low = dot(old_inverse, cross, ((1,), (0,)))
    schur = ridge_shift * block + square - dot(cross_low, cross_low, ((0,), (0,)))
    schur_inverse = factor_single(schur)

    def solve(old_side, new_side):
        up = dot(old_inverse, old_side, ((1,), (0,)))
        down = dot(schur_inverse, new_side - dot(cross_low, up, ((0,), (0,))), ((1,), (0,)))
        new_coef = dot(schur_inverse, down, ((0,), (0,)))
        old_coef = dot(old_inverse, up - dot(cross_low, new_coef, ((1,), (0,))), ((0,), (0,)))
        return old_coef, new_coef

    def apply(vector, coefs):
        fitted = dot(old_full, coefs[0], ((1,), (0,))) + dot(columns, coefs[1], ((1,), (0,)))
        return (vector - fitted) / ridge_shift

    direction = apply(targets, solve(old_proj, new_proj))
    weights = spread(lax.dynamic_slice_in_dim(direction, part * half, half, 0), parts)
    weights = lax.dynamic_index_in_dim(weights.reshape(chips, 2, half), part, 1, False)
    rows_part = kernel_rows(points, norms, others, point_norms(others), weights.reshape(-1))

    image_part = rows_part + (0.5 * ridge_shift) * direction
    sums = jnp.concatenate(
        [
            dot(image_part, old_full, ((0,), (0,))),
            dot(image_part, columns, ((0,), (0,))),
            jnp.sum(direction * image_part)[None],
            0.5 * jnp.sum(direction * targets)[None],
            jnp.zeros((126,), f32),
        ]
    )
    sums = jnp.sum(spread(sums, parts), axis=0)
    image = rows_part + swap(rows_part) + ridge_shift * direction
    alpha = sums[prev + pivot_count + 1] / sums[prev + pivot_count]
    residual = targets - alpha * image
    coefs = solve(old_proj - alpha * sums[:prev], new_proj - alpha * sums[prev : prev + pivot_count])
    preconditioned = apply(residual, coefs)
    mine = lax.dynamic_slice_in_dim(block_inverse, part * cols, cols, 0)
    new_part = dot(columns, mine, ((1,), (1,)))
    return new_part, alpha * direction, residual, preconditioned


def solution(mesh):
    in_specs = (P("rows", None), P("rows", "sub"), P("rows"), P())
    out_specs = (P("rows", "sub"), P("rows"), P("rows"), P("rows"))
    return jax.shard_map(local, mesh=mesh, in_specs=in_specs, out_specs=out_specs, check_vma=False)
```

time: 1850 us -> 400 us (0.22)
  blocking collectives: 699 us -> 0 us
  other arithmetic: 472 us -> 49.6 us
  matrix products: 296 us -> 41.1 us
  waiting for transfers between devices: 273 us -> 103 us
  Pallas kernels: 0 us -> 79.8 us
  starting transfers between devices: 0.38 us -> 50.4 us
  local copies, waits for them, and re-layouts: 72 us -> 51 us
    psum x4 -> x0, blocking collectives: 523 us -> none  [the longest x1 175 us: local(): gram_part, proj_part = lax.psum((gram_part, proj_part), 'rows')]
    another operation x52 -> x1, other arithmetic: 388 us -> 0.02 us  [kernel_rows(): extra = jnp.pad(jnp.stack(pieces, axis=1), ((0, 0), (0, dim - 3)))]
    psum x2 -> x0, waiting for transfers between devices: 259 us -> none  [the longest x1 130 us: local(): gram_part, proj_part = lax.psum((gram_part, proj_part), 'rows')]
    all_gather x2 -> x0, blocking collectives: 175 us -> none  [the longest x1 173 us: local(): direction_full = lax.all_gather(direction, 'rows', axis=0, tiled=True)]
    another operation x87 -> x0, matrix products: 105 us -> none  [the longest x60 67.9 us: precondition(): coef = jax.scipy.linalg.cho_solve((core_lower, True), projection)]
    all_to_all x0 -> x8, waiting for transfers between devices: none -> 101 us  [exchange(): return lax.all_to_all(pieces, everyone, 0, 0, tiled=True)]
    dot_general x66 -> x2, matrix products: 89.7 us -> 0.9 us  [kernel_values(): lax.dot_general(left, right, (((1,), (1,)), ((), ())), preferred_element_...]
    pallas_call x0 -> x3, Pallas kernels: none -> 79.8 us  [the longest x1 38.1 us: factor_pair(): pl.pallas_call(pair_kernel, out_shape=(shape, shape), compiler_params=plt...]
  transfers between devices with their start and end apart: 5 -> 12, of which waited for: 3 -> 9; matrix products, arithmetic and copies ran while one was open for 21% -> 28% of each run, Pallas kernels for 0% -> 16%
where the time goes in v1:
time: 400 us; the launch traced here: 392 us
  waiting for transfers between devices  103 us (26%)
  Pallas kernels  79.8 us (20%)
  local copies, waits for them, and re-layouts  51 us (13%)
  starting transfers between devices  50.4 us (13%)
  other arithmetic  49.6 us (12%)
  matrix products  41.1 us (10%)
  between operations  17.4 us (4%)
    all_to_all x8, waiting for transfers between devices, exchange(): return lax.all_to_all(pieces, everyone, 0, 0, tiled=True)  101 us
    all_to_all x8, starting transfers between devices, exchange(): return lax.all_to_all(pieces, everyone, 0, 0, tiled=True)  49.4 us
    dot_general x25, matrix products, dot(): lax.dot_general(left, right, (contract, ((), ())), precision=precise, pre...  39 us
    pallas_call x1, Pallas kernels, factor_pair(): pl.pallas_call(pair_kernel, out_shape=(shape, shape), compiler_params=plt...  38.1 us
    pallas_call x1, Pallas kernels, factor_single(): pl.pallas_call(single_kernel, out_shape=jax.ShapeDtypeStruct(matrix.shape...  23.5 us
    all_to_all x6, other arithmetic, exchange(): return lax.all_to_all(pieces, everyone, 0, 0, tiled=True)  22.4 us
    pallas_call x1, Pallas kernels, kernel_rows(): pl.pallas_call(lambda *refs: rows_kernel(scale, *refs), grid=(steps,), in...  18.2 us
    all_to_all x6, local copies, waits for them, and re-layouts, exchange(): return lax.all_to_all(pieces, everyone, 0, 0, tiled=True)  10.9 us
  transfers between devices with their start and end apart: 12, of which 9 were waited for; matrix products, arithmetic and copies ran while one was open for 28% of the time, Pallas kernels for 16%

profile of v1, /device:TPU:8, one launch (start us, length us, event | category | flops | bytes accessed | tf_op | source)
XLA Modules:
  0.0 392.1 jit_solution(3708847128958833473)
XLA Ops:
  7.2 1.3 reduce-precision_convert_fusion
  8.6 1.2 fusion.12
  11.7 4.2 %reduce.31 = bf16[128,2304]{1,0:T(8,128)(2,1)S(1)} reduce(bf16[128,1,2304]{2,1,0:T(2,128)(2,1)S(1)} %all_to_all.52, bf16[]{:T(256)} %broadcast.111), dimensions={1}, to_apply=%all_to_all.52.reduce_sub_computation | reduce | bytes 1179650 | tf_op jit(solution)/shard_map/all_to_all | solution.py:185
  16.8 10.5 %all-to-all-start = ((bf16[128,2,1152]{2,1,0:T(2,128)(2,1)}), bf16[128,2,1152]{2,1,0:T(2,128)(2,1)S(1)}, u32[]{:S(2)}, u32[]{:S(2)}) async-start(bf16[128,2,1152]{2,1,0:T(2,128)(2,1)} %reshape.231), calls=%async_computation | async-start | bytes 1179648 | tf_op jit(solution)/shard_map/all_to_all | solution.py:185
  28.0 12.9 %all-to-all-done = bf16[128,2,1152]{2,1,0:T(2,128)(2,1)S(1)} async-done(((bf16[128,2,1152]{2,1,0:T(2,128)(2,1)}), bf16[128,2,1152]{2,1,0:T(2,128)(2,1)S(1)}, u32[]{:S(2)}, u32[]{:S(2)}) %all-to-all-start) | async-done | bytes 589856 | tf_op jit(solution)/shard_map/all_to_all | solution.py:185
  41.7 3.6 reduce.2
  46.4 1.2 broadcast_in_dim.21
  47.6 8.2 %reduce.32 = bf16[128,4608]{1,0:T(8,128)(2,1)S(1)} reduce(bf16[128,1,4608]{2,1,0:T(2,128)(2,1)S(1)} %broadcast_in_dim.21, bf16[]{:T(256)} %broadcast.111), dimensions={1}, to_apply=%broadcast_in_dim.21.reduce_sub_computation | reduce | bytes 2359298 | tf_op jit(solution)/shard_map/broadcast_in_dim | solution.py:189
  55.8 1.2 reshape.233
  57.0 5.2 %all-to-all-start.1 = ((bf16[128,2,2304]{2,1,0:T(2,128)(2,1)}), bf16[128,2,2304]{2,1,0:T(2,128)(2,1)S(1)}, u32[]{:S(2)}, u32[]{:S(2)}) async-start(bf16[128,2,2304]{2,1,0:T(2,128)(2,1)} %reshape.233), calls=%async_computation.1 | async-start | bytes 2359296 | tf_op jit(solution)/shard_map/all_to_all | solution.py:185
  63.4 1.6 collective-permute-done
  65.1 1.5 broadcast_select_fusion.3
  66.6 19.3 %all-to-all-done.1 = bf16[128,2,2304]{2,1,0:T(2,128)(2,1)S(1)} async-done(((bf16[128,2,2304]{2,1,0:T(2,128)(2,1)}), bf16[128,2,2304]{2,1,0:T(2,128)(2,1)S(1)}, u32[]{:S(2)}, u32[]{:S(2)}) %all-to-all-start.1) | async-done | bytes 1179680 | tf_op jit(solution)/shard_map/all_to_all | solution.py:185
  85.9 3.4 reshape.234
  89.3 9.3 %reduce.3 = bf16[128,4608]{1,0:T(8,128)(2,1)} reduce(bf16[128,1,4608]{2,1,0:T(2,128)(2,1)} %reshape.234, bf16[]{:T(256)} %constant.61), dimensions={1}, to_apply=%all_to_all.42.reduce_sub_computation | reduce | bytes 2359298 | tf_op jit(solution)/shard_map/all_to_all | solution.py:185
  98.6 2.0 reshape.160
  101.6 3.3 multiply_reduce_fusion.1
  105.1 3.8 fusion.6
  108.9 2.7 reshape.163
  111.6 1.3 select_maximum_fusion
  112.9 1.9 all_to_all.46
  114.8 5.8 %all-to-all-start.4 = ((f32[128,1,2176]{2,1,0:T(1,128)}), f32[128,1,2176]{2,1,0:T(1,128)S(1)}, u32[]{:S(2)}, u32[]{:S(2)}) async-start(f32[128,1,2176]{2,1,0:T(1,128)} %all_to_all.46), calls=%async_computation.4 | async-start | bytes 2228224 | tf_op jit(solution)/shard_map/all_to_all | solution.py:185
  120.6 2.2 fusion.43
  122.8 2.4 all_to_all.53
  125.2 14.7 %all-to-all-done.4 = f32[128,1,2176]{2,1,0:T(1,128)S(1)} async-done(((f32[128,1,2176]{2,1,0:T(1,128)}), f32[128,1,2176]{2,1,0:T(1,128)S(1)}, u32[]{:S(2)}, u32[]{:S(2)}) %all-to-all-start.4) | async-done | bytes 1114144 | tf_op jit(solution)/shard_map/all_to_all | solution.py:185
  139.9 6.5 %all-to-all-start.2 = ((f32[128,1,1024]{2,1,0:T(1,128)}), f32[128,1,1024]{2,1,0:T(1,128)}, u32[]{:S(2)}, u32[]{:S(2)}) async-start(f32[128,1,1024]{2,1,0:T(1,128)} %all_to_all.53), calls=%async_computation.2 | async-start | bytes 1048576 | tf_op jit(solution)/shard_map/all_to_all | solution.py:185
  146.4 2.6 reduce.5
  150.4 2.7 all_to_all.48
  153.2 5.9 %all-to-all-done.2 = f32[128,1,1024]{2,1,0:T(1,128)} async-done(((f32[128,1,1024]{2,1,0:T(1,128)}), f32[128,1,1024]{2,1,0:T(1,128)}, u32[]{:S(2)}, u32[]{:S(2)}) %all-to-all-start.2) | async-done | bytes 524320 | tf_op jit(solution)/shard_map/all_to_all | solution.py:185
  159.1 5.0 %all-to-all-start.5 = ((f32[128,1,2176]{2,1,0:T(1,128)}), f32[128,1,2176]{2,1,0:T(1,128)S(1)}, u32[]{:S(2)}, u32[]{:S(2)}) async-start(f32[128,1,2176]{2,1,0:T(1,128)} %all_to_all.48), calls=%async_computation.5 | async-start | bytes 2228224 | tf_op jit(solution)/shard_map/all_to_all | solution.py:185
  164.1 2.3 reduce.4
  166.9 16.5 %all-to-all-done.5 = f32[128,1,2176]{2,1,0:T(1,128)S(1)} async-done(((f32[128,1,2176]{2,1,0:T(1,128)}), f32[128,1,2176]{2,1,0:T(1,128)S(1)}, u32[]{:S(2)}, u32[]{:S(2)}) %all-to-all-start.5) | async-done | bytes 1114144 | tf_op jit(solution)/shard_map/all_to_all | solution.py:185
  183.4 1.6 broadcast_in_dim.23
  185.0 5.1 %all-to-all-start.3 = ((f32[128,1,2048]{2,1,0:T(1,128)}), f32[128,1,2048]{2,1,0:T(1,128)S(1)}, u32[]{:S(2)}, u32[]{:S(2)}) async-start(f32[128,1,2048]{2,1,0:T(1,128)} %broadcast_in_dim.23), calls=%async_computation.3 | async-start | bytes 2097152 | tf_op jit(solution)/shard_map/all_to_all | solution.py:185
  190.8 3.5 select_add_fusion.second_in
  194.3 14.4 %all-to-all-done.3 = f32[128,1,2048]{2,1,0:T(1,128)S(1)} async-done(((f32[128,1,2048]{2,1,0:T(1,128)}), f32[128,1,2048]{2,1,0:T(1,128)S(1)}, u32[]{:S(2)}, u32[]{:S(2)}) %all-to-all-start.3) | async-done | bytes 1048608 | tf_op jit(solution)/shard_map/all_to_all | solution.py:185
  208.7 2.4 copy.50
  211.0 2.1 fusion.46
  213.1 1.3 copy.52
  215.8 1.2 select_add_fusion.1.first_in
  217.0 38.1 %factor_pair.1 = (f32[512,512]{1,0:T(8,128)S(1)}, f32[512,512]{1,0:T(8,128)S(1)}) custom-call(f32[512,512]{1,0:T(8,128)S(1)} %select_add_fusion.1.first_in, f32[512,512]{1,0:T(8,128)S(1)} %select_add_fusion.second_in), custom_call_target="tpu_custom_call" | custom-call | tf_op jit(solution)/shard_map/factor_pair/pallas_call | solution.py:95
  255.1 3.2 broadcast_select_fusion
  258.3 1.1 copy-done.19
  259.8 8.0 %slice_reduce_fusion = (f32[128,2048]{1,0:T(8,128)S(1)}, f32[128,2048]{1,0:T(8,128)}) fusion(f32[1,128,2176]{2,0,1:T(1,128)} %copy-done.19, f32[1,128,2176]{2,0,1:T(1,128)} %copy-done.20), kind=kLoop, calls=%fused_computation.37 | loop fusion | bytes 4194304 | tf_op jit(solution)/shard_map/slice | solution.py:278
  267.8 2.6 squeeze.28
  270.4 1.3 squeeze.29
  271.7 3.1 fusion.49
  274.8 1.9 fusion.50
  277.0 23.5 %factor_single.1 = f32[512,512]{1,0:T(8,128)S(1)} custom-call(f32[512,512]{1,0:T(8,128)S(1)} %add_subtract_fusion.matrix), custom_call_target="tpu_custom_call" | custom-call | tf_op jit(solution)/shard_map/factor_single/pallas_call | solution.py:104
  300.7 1.0 fusion.48
  302.4 1.0 convolution_bitcast_fusion.5
  304.0 1.0 fusion.51
  308.5 5.4 %all-to-all-start.6 = ((f32[128,1,384]{2,1,0:T(1,128)}), f32[128,1,384]{2,1,0:T(1,128)S(1)}, u32[]{:S(2)}, u32[]{:S(2)}) async-start(f32[128,1,384]{2,1,0:T(1,128)} %broadcast_in_dim.26), calls=%async_computation.6 | async-start | bytes 393216 | tf_op jit(solution)/shard_map/all_to_all | solution.py:185
  314.2 9.4 %all-to-all-done.6 = f32[128,1,384]{2,1,0:T(1,128)S(1)} async-done(((f32[128,1,384]{2,1,0:T(1,128)}), f32[128,1,384]{2,1,0:T(1,128)S(1)}, u32[]{:S(2)}, u32[]{:S(2)}) %all-to-all-start.6) | async-done | bytes 196640 | tf_op jit(solution)/shard_map/all_to_all | solution.py:185
  324.3 5.8 %multiply_reduce_fusion = f32[24576]{0:T(1024)S(1)} fusion(bf16[24576,128]{1,0:T(8,128)(2,1)} %all-gather.2.cloned.1.call-done.refs_1_), kind=kLoop, calls=%fused_computation | loop fusion | flops 9412608 | bytes 6389760 | tf_op jit(solution)/shard_map/reduce_sum | solution.py:177
  330.2 18.2 %kernel_rows.1 = f32[8,768]{1,0:T(8,128)S(1)} custom-call(bf16[768,256]{1,0:T(8,128)(2,1)S(1)} %fusion.27.refs_0_, bf16[24576,128]{1,0:T(8,128)(2,1)S(1)} %copy-done, f32[1,24576]{1,0:T(1,128)S(1)} %bitcast.111, f32[1,24576]{1,0:T(1,128)S(1)} %bitcast.110), custom_call_target="tpu_custom_call" | custom-call | tf_op jit(solution)/shard_map/kernel_rows/pallas_call | solution.py:151
  349.0 1.4 fusion.42
  350.4 1.4 fusion.52
  353.2 1.2 broadcast_in_dim.57
  354.4 6.0 %all-to-all-start.7 = ((f32[128,1,1152]{2,1,0:T(1,128)}), f32[128,1,1152]{2,1,0:T(1,128)}, u32[]{:S(2)}, u32[]{:S(2)}) async-start(f32[128,1,1152]{2,1,0:T(1,128)} %broadcast_in_dim.57), calls=%async_computation.7 | async-start | bytes 1179648 | tf_op jit(solution)/shard_map/all_to_all | solution.py:185
  360.4 4.9 %fusion.25 = f32[768,256]{1,0:T(8,128)} fusion(f32[768,512]{0,1:T(8,128)} %copy-done.3, f32[512,512]{1,0:T(8,128)S(1)} %copy-done.2, s32[]{:T(128)S(6)} %select_n.50), kind=kOutput, calls=%fused_computation.53 | convolution fusion | flops 1207959552 | bytes 2883588 | tf_op jit(solution)/shard_map/dot_general | solution.py:181
  366.0 7.9 %all-to-all-done.7 = f32[128,1,1152]{2,1,0:T(1,128)} async-done(((f32[128,1,1152]{2,1,0:T(1,128)}), f32[128,1,1152]{2,1,0:T(1,128)}, u32[]{:S(2)}, u32[]{:S(2)}) %all-to-all-start.7) | async-done | bytes 589856 | tf_op jit(solution)/shard_map/all_to_all | solution.py:185
  373.9 1.4 reduce_sum.102
  380.6 1.0 fusion.54
  (146 shorter events, 27.3 us)
Async XLA Ops:
  7.2 1.3 copy-start.22
  7.2 1.5 copy-start.33
  16.8 24.1 %all-to-all-start = ((bf16[128,2,1152]{2,1,0:T(2,128)(2,1)}), bf16[128,2,1152]{2,1,0:T(2,128)(2,1)S(1)}, u32[]{:S(2)}, u32[]{:S(2)}) async-start(bf16[128,2,1152]{2,1,0:T(2,128)(2,1)} %reshape.231), calls=%async_computation | async-start | bytes 1179648 | tf_op jit(solution)/shard_map/all_to_all | solution.py:185
  27.3 297.0 %all-gather.2.cloned.1.call-start = ((), (), s32[]{:S(2)}) async-start(), calls=%async_computation.8 | async-start | bytes 6389760 | tf_op jit(solution)/shard_map/all_gather | solution.py:219
  57.0 5.2 %copy-start.17 = (f32[768,256]{1,0:T(8,128)S(1)}, f32[768,256]{1,0:T(8,128)}, u32[]{:S(2)}) copy-start(f32[768,256]{1,0:T(8,128)} %param.5) | copy-start | bytes 2359300
  57.0 5.8 %copy-start.23 = (bf16[768,128]{1,0:T(8,128)(2,1)S(1)}, bf16[768,128]{1,0:T(8,128)(2,1)}, u32[]{:S(2)}) copy-start(bf16[768,128]{1,0:T(8,128)(2,1)} %param.4) | copy-start | bytes 589828
  57.0 28.8 %all-to-all-start.1 = ((bf16[128,2,2304]{2,1,0:T(2,128)(2,1)}), bf16[128,2,2304]{2,1,0:T(2,128)(2,1)S(1)}, u32[]{:S(2)}, u32[]{:S(2)}) async-start(bf16[128,2,2304]{2,1,0:T(2,128)(2,1)} %reshape.233), calls=%async_computation.1 | async-start | bytes 2359296 | tf_op jit(solution)/shard_map/all_to_all | solution.py:185
  62.6 0.9 copy-start.25
  62.6 2.5 collective-permute-start
  66.5 54.0 %copy-start.9 = (f32[768,256]{0,1:T(8,128)}, f32[768,256]{0,1:T(8,128)S(1)}, u32[]{:S(2)}) copy-start(f32[768,256]{0,1:T(8,128)S(1)} %get-tuple-element.16) | copy-start | bytes 2359300
  66.6 54.0 %copy-start.13 = (f32[768,256]{0,1:T(8,128)}, f32[768,256]{0,1:T(8,128)S(1)}, u32[]{:S(2)}) copy-start(f32[768,256]{0,1:T(8,128)S(1)} %get-tuple-element.17) | copy-start | bytes 2359300
  100.7 0.9 copy-start.28
  100.7 0.9 copy-start.30
  100.9 0.7 copy-start.32
  101.2 3.8 copy-start.26
  101.2 3.8 copy-start.27
  105.0 3.9 copy-start.3
  114.8 5.8 %copy-start.18 = (f32[768,256]{1,0:T(8,128)S(1)}, f32[768,256]{1,0:T(8,128)}, u32[]{:S(2)}) copy-start(f32[768,256]{1,0:T(8,128)} %param.5) | copy-start | bytes 2359300
  114.8 25.2 %all-to-all-start.4 = ((f32[128,1,2176]{2,1,0:T(1,128)}), f32[128,1,2176]{2,1,0:T(1,128)S(1)}, u32[]{:S(2)}, u32[]{:S(2)}) async-start(f32[128,1,2176]{2,1,0:T(1,128)} %all_to_all.46), calls=%async_computation.4 | async-start | bytes 2228224 | tf_op jit(solution)/shard_map/all_to_all | solution.py:185
  139.9 19.2 %all-to-all-start.2 = ((f32[128,1,1024]{2,1,0:T(1,128)}), f32[128,1,1024]{2,1,0:T(1,128)}, u32[]{:S(2)}, u32[]{:S(2)}) async-start(f32[128,1,1024]{2,1,0:T(1,128)} %all_to_all.53), calls=%async_computation.2 | async-start | bytes 1048576 | tf_op jit(solution)/shard_map/all_to_all | solution.py:185
  159.1 24.3 %all-to-all-start.5 = ((f32[128,1,2176]{2,1,0:T(1,128)}), f32[128,1,2176]{2,1,0:T(1,128)S(1)}, u32[]{:S(2)}, u32[]{:S(2)}) async-start(f32[128,1,2176]{2,1,0:T(1,128)} %all_to_all.48), calls=%async_computation.5 | async-start | bytes 2228224 | tf_op jit(solution)/shard_map/all_to_all | solution.py:185
  183.4 6.9 %copy-start.29 = (bf16[512,64]{1,0:T(8,128)(2,1)S(1)}, bf16[512,64]{1,0:T(8,128)(2,1)}, u32[]{:S(2)}) copy-start(bf16[512,64]{1,0:T(8,128)(2,1)} %copy-done.28) | copy-start | bytes 196612
  183.4 6.9 %copy-start.31 = (bf16[512,64]{1,0:T(8,128)(2,1)S(1)}, bf16[512,64]{1,0:T(8,128)(2,1)}, u32[]{:S(2)}) copy-start(bf16[512,64]{1,0:T(8,128)(2,1)} %copy-done.30) | copy-start | bytes 196612
  185.0 23.7 %all-to-all-start.3 = ((f32[128,1,2048]{2,1,0:T(1,128)}), f32[128,1,2048]{2,1,0:T(1,128)S(1)}, u32[]{:S(2)}, u32[]{:S(2)}) async-start(f32[128,1,2048]{2,1,0:T(1,128)} %broadcast_in_dim.23), calls=%async_computation.3 | async-start | bytes 2097152 | tf_op jit(solution)/shard_map/all_to_all | solution.py:185
  190.1 65.0 %collective-permute-start.1 = (f32[1,128,2176]{2,0,1:T(1,128)S(1)}, f32[1,128,2176]{2,0,1:T(1,128)}, u32[]{:S(2)}, u32[]{:S(2)}) collective-permute-start(f32[1,128,2176]{2,0,1:T(1,128)S(1)} %bitcast.112), channel_id=1, source_target_pairs={{0,1},{1,0},{2,3},{3,2},{4,5},{5,4},{6,7},{7,6},{8,9},{9,8},{10,11... | collective-permute-start | bytes 3342344 | tf_op jit(solution)/shard_map/ppermute | solution.py:193
  255.1 3.2 copy-start.1
  258.3 1.1 copy-start.19
  258.3 1.5 copy-start.20
  274.8 29.2 %copy-start.7 = (f32[512,512]{1,0:T(8,128)}, f32[512,512]{1,0:T(8,128)S(1)}, u32[]{:S(2)}) copy-start(f32[512,512]{1,0:T(8,128)S(1)} %fusion.49) | copy-start | bytes 3145732
  274.8 1.9 copy-start.21
  303.3 2.3 copy-start.10
  303.4 2.3 copy-start.14
  305.0 1.6 copy-start.4
  306.6 7.5 %copy-start.24 = (bf16[768,128]{1,0:T(8,128)(2,1)S(1)}, bf16[768,128]{1,0:T(8,128)(2,1)}, u32[]{:S(2)}) copy-start(bf16[768,128]{1,0:T(8,128)(2,1)} %param.4) | copy-start | bytes 589828
  308.5 15.1 %all-to-all-start.6 = ((f32[128,1,384]{2,1,0:T(1,128)}), f32[128,1,384]{2,1,0:T(1,128)S(1)}, u32[]{:S(2)}, u32[]{:S(2)}) async-start(f32[128,1,384]{2,1,0:T(1,128)} %broadcast_in_dim.26), calls=%async_computation.6 | async-start | bytes 393216 | tf_op jit(solution)/shard_map/all_to_all | solution.py:185
  324.3 5.9 %copy-start = (bf16[24576,128]{1,0:T(8,128)(2,1)S(1)}, bf16[24576,128]{1,0:T(8,128)(2,1)}, u32[]{:S(2)}) copy-start(bf16[24576,128]{1,0:T(8,128)(2,1)} %all-gather.2.cloned.1.call-done.refs_1_) | copy-start | bytes 18874372
  330.1 18.9 %copy-start.11 = (f32[768,256]{0,1:T(8,128)S(1)}, f32[768,256]{0,1:T(8,128)}, u32[]{:S(2)}) copy-start(f32[768,256]{0,1:T(8,128)} %copy-done.9) | copy-start | bytes 2359300
  330.1 18.9 %copy-start.15 = (f32[768,256]{0,1:T(8,128)S(1)}, f32[768,256]{0,1:T(8,128)}, u32[]{:S(2)}) copy-start(f32[768,256]{0,1:T(8,128)} %copy-done.13) | copy-start | bytes 2359300
  348.4 2.1 copy-start.5
  350.4 10.0 %copy-start.2 = (f32[512,512]{1,0:T(8,128)S(1)}, f32[512,512]{1,0:T(8,128)}, u32[]{:S(2)}) copy-start(f32[512,512]{1,0:T(8,128)} %copy-done.1) | copy-start | bytes 3145732
  354.4 19.4 %all-to-all-start.7 = ((f32[128,1,1152]{2,1,0:T(1,128)}), f32[128,1,1152]{2,1,0:T(1,128)}, u32[]{:S(2)}, u32[]{:S(2)}) async-start(f32[128,1,1152]{2,1,0:T(1,128)} %broadcast_in_dim.57), calls=%async_computation.7 | async-start | bytes 1179648 | tf_op jit(solution)/shard_map/all_to_all | solution.py:185
  365.3 12.9 %copy-start.8 = (f32[512,512]{1,0:T(8,128)S(1)}, f32[512,512]{1,0:T(8,128)}, u32[]{:S(2)}) copy-start(f32[512,512]{1,0:T(8,128)} %copy-done.7) | copy-start | bytes 3145732
  365.4 18.7 %collective-permute-start.2 = (f32[768]{0:T(1024)S(1)}, f32[768]{0:T(1024)S(1)}, u32[]{:S(2)}, u32[]{:S(2)}) collective-permute-start(f32[768]{0:T(1024)S(1)} %slice_reduce_fusion.3), channel_id=1, source_target_pairs={{0,1},{1,0},{2,3},{3,2},{4,5},{5,4},{6,7},{7,6},{8,9},{9,8},{10,11... | collective-permute-start | bytes 9224 | tf_op jit(solution)/shard_map/ppermute | solution.py:193
  378.9 2.6 copy-start.6
  381.6 1.6 copy-start.12
  381.6 1.6 copy-start.16
Sparse Core Ops, SparseCore 0:
  30.9 81.8 all-gather.1
